TPU v7x, 32 devices: a whole 2x2x4 slice. The times are simulated.
32 devices in a mesh: section: 8 (over z, core), mp: 4 (over y, x).
Axes of the slice: x: 2, y: 2, z: 4, core: 2. Of those that a mesh axis runs over, the one named last changes fastest.
Arguments:
- matches: int32 [1024, 2], P('section'), may hold values from 0 to 7, all different within a row; in each aligned block of 128 rows (0 to 127, 128 to 255, ...) at most 64 rows name the same one
- actions: int32 [2, 1024, 2], P(None, 'section'), may hold values from 0 to 1023
- state: float32 [1024, 2, 2048], P('section', None, 'mp'), may hold values from -6 to 6
- embed: bfloat16 [1024, 2048], P(None, 'mp'), may hold values from -3 to 3
- w_in: bfloat16 [8, 1, 2048, 8192], P('section', None, None, 'mp'), may hold values from -0.125 to 0.125
- w_out: bfloat16 [8, 1, 8192, 2048], P('section', None, 'mp'), may hold values from -0.0625 to 0.0625
- head: bfloat16 [8, 2048, 1024], P('section', None, 'mp'), may hold values from -16 to 16
Outputs:
- logp: float32 [2, 1024, 2], P(None, 'section')
Inputs may be any that keep to these rules, and one draw needn't show every extreme that they name: `matches`: each game names two different agents; among the 128 games of one index of section no agent is named more than 64 times, a bound that some block reaches in some of these groups.
All inputs are finite; a program needn't handle non-finite values.
Results may differ from a plain program's by a relative error of at most 0.0095.
Values may be sent and summed in bfloat16 or wider, within the bound.
No kernel may reach another device: no remote copies, remote signals or barrier semaphores. Data moves between devices by JAX's collectives and lax.ppermute only.
A program may use at most 64 MiB of HBM per device.

v0:
```python
import jax
import jax.numpy as jnp
from jax import lax
from jax.sharding import PartitionSpec as P

STEPS = 2


norm_eps = 1e-06


def rms_round(source):
    widened = source.astype(jnp.float32)
    scale = lax.rsqrt(jnp.mean(widened * widened, axis=-1, keepdims=True) + norm_eps)
    return (widened * scale).astype(jnp.bfloat16)


def per_device(matches, actions, state, embed, w_in, w_out, head):
    sections = lax.axis_size("section")
    game_count = matches.shape[0]
    feat_width = state.shape[2]
    slot_cap = 4 * game_count // sections
    served = sections * slot_cap
    owners = matches.reshape(-1)
    onehot = (owners[:, None] == jnp.arange(sections, dtype=jnp.int32)[None, :]).astype(jnp.int32)
    slot_of = jnp.sum((jnp.cumsum(onehot, axis=0) - onehot) * onehot, axis=1)
    action_width = head.shape[2]
    columns = lax.axis_index("mp") * action_width + jnp.arange(action_width, dtype=jnp.int32)
    current = state
    results = []
    for step_idx in range(STEPS):
        observed = current.astype(jnp.bfloat16).reshape(2 * game_count, feat_width)
        outgoing = (
            jnp.zeros((sections, slot_cap, feat_width), jnp.bfloat16)
            .at[owners, slot_of]
            .set(observed)
        )
        arrived = lax.all_to_all(outgoing, "section", split_axis=0, concat_axis=0, tiled=True)
        inputs = lax.all_gather(arrived.reshape(served, feat_width), "mp", axis=1, tiled=True)
        summed = inputs.astype(jnp.float32)
        normed = rms_round(inputs)
        hidden = jax.nn.gelu(
            jnp.dot(normed, w_in[0, 0], preferred_element_type=jnp.float32)
        ).astype(jnp.bfloat16)
        partial_value = jnp.dot(hidden, w_out[0, 0], preferred_element_type=jnp.float32)
        summed = inputs.astype(jnp.float32) + lax.psum(
            partial_value.astype(jnp.bfloat16), "mp"
        ).astype(jnp.float32)
        logits = jnp.dot(rms_round(summed), head[0], preferred_element_type=jnp.float32)
        returned = lax.all_to_all(
            logits.reshape(sections, slot_cap, action_width).astype(jnp.bfloat16),
            "section",
            split_axis=0,
            concat_axis=0,
            tiled=True,
        ).astype(jnp.float32)
        row_logits = returned[owners, slot_of]
        row_peak = lax.pmax(jnp.max(row_logits, axis=1), "mp")
        chosen = actions[step_idx].reshape(-1)
        local_total = jnp.sum(jnp.exp(row_logits - row_peak[:, None]), axis=1)
        local_pick = jnp.sum(
            jnp.where(columns[None, :] == chosen[:, None], row_logits, 0.0), axis=1
        )
        row_total, picked = lax.psum((local_total, local_pick), "mp")
        results.append((picked - row_peak - jnp.log(row_total)).reshape(game_count, 2))
        picked_rows = jnp.take(embed, actions[step_idx], axis=0).astype(jnp.float32)
        current = 0.8 * current + picked_rows + 0.5 * picked_rows[:, ::-1, :]
    return jnp.stack(results)


def solution(mesh):
    return jax.shard_map(
        per_device,
        mesh=mesh,
        in_specs=(
            P("section", None),
            P(None, "section", None),
            P("section", None, "mp"),
            P(None, "mp"),
            P("section", None, None, "mp"),
            P("section", None, "mp", None),
            P("section", None, "mp"),
        ),
        out_specs=P(None, "section", None),
        check_vma=False,
    )
```

profile of v0, /device:TPU:0, one launch (start us, length us, event | category | flops | bytes accessed | tf_op | source)
XLA Modules:
  0.0 325.1 jit_solution(18214923491018854760)
XLA Ops:
  6.5 0.0 copy-start
  6.5 0.9 copy.18
  7.4 0.1 eq.61
  7.6 0.1 eq.57
  7.7 0.1 reshape.151
  7.9 0.7 compare_select_fusion.2
  8.6 0.7 compare_and_fusion
  9.2 0.6 reduce-window.6
  9.8 0.2 slice_reduce_fusion
  10.1 0.1 copy.23
  10.2 0.1 reshape.165
  10.4 2.6 gather_fusion.1
  12.9 0.1 reshape.164
  13.0 0.1 copy.22
  13.2 0.3 fusion.60
  13.5 1.4 rev.3
  15.0 0.8 fusion.74
  15.8 0.1 reshape.179
  15.9 0.1 fusion.62
  16.0 13.8 %scatter_fusion = bf16[8,64,512]{2,1,0:T(8,128)(2,1)S(1)} fusion(bf16[8,64,512]{2,1,0:T(8,128)(2,1)S(1)} %broadcast.146.clone.1, s32[256]{0:T(256)S(1)} %bitcast.53, bf16[256,512]{1,0:T(8,128)(2,1)S(1)} %reshape.179), kind=kCustom, calls=%fused_computation.3 | custom fusion | bytes 788480 | tf_op jit(solution)/shard_map/scatter | solution.py:36
  29.8 21.6 %all_to_all.20 = bf16[8,64,512]{2,1,0:T(8,128)(2,1)} all-to-all(bf16[8,64,512]{2,1,0:T(8,128)(2,1)S(1)} %scatter_fusion), channel_id=1, replica_groups=mesh['section'=8,'mp'=4] {'section'}, dimensions={0} | all-to-all | bytes 1048576 | tf_op jit(solution)/shard_map/all_to_all | solution.py:38
  51.4 0.0 all-gather.3.cloned.1.call-update
  51.4 0.0 all-gather.5.cloned.1.call-start
  51.5 0.1 reshape.185
  51.6 13.8 %scatter_fusion.1 = bf16[8,64,512]{2,1,0:T(8,128)(2,1)S(1)} fusion(bf16[8,64,512]{2,1,0:T(8,128)(2,1)S(1)} %broadcast.146.clone, s32[256]{0:T(256)S(1)} %bitcast.54, bf16[256,512]{1,0:T(8,128)(2,1)S(1)} %reshape.185), kind=kCustom, calls=%fused_computation.4 | custom fusion | bytes 788480 | tf_op jit(solution)/shard_map/scatter | solution.py:36
  65.4 18.4 %all_to_all.21 = bf16[8,64,512]{2,1,0:T(8,128)(2,1)} all-to-all(bf16[8,64,512]{2,1,0:T(8,128)(2,1)S(1)} %scatter_fusion.1), channel_id=1, replica_groups=mesh['section'=8,'mp'=4] {'section'}, dimensions={0} | all-to-all | bytes 1048576 | tf_op jit(solution)/shard_map/all_to_all | solution.py:38
  83.9 0.0 all-gather.5.cloned.1.call-update
  83.9 0.2 all-reduce.5.cloned.1.call-start
  84.1 1.5 all-gather.3.cloned.1.call-done
  85.7 2.2 fusion.8
  87.9 34.8 %all-gather.5.cloned.1.call-done = bf16[512,2048]{1,0:T(8,128)(2,1)} async-done(((bf16[512,512]{1,0:T(8,128)(2,1)}), bf16[512,2048]{1,0:T(8,128)(2,1)}) %all-gather.5.cloned.1.call-update) | async-done | bytes 2097168 | tf_op jit(solution)/shard_map/all_gather | solution.py:39
  122.7 2.1 fusion.18
  124.8 0.0 copy-done.1
  124.8 16.1 %fusion.28 = bf16[512,2048]{1,0:T(8,128)(2,1)} fusion(bf16[1,1,2048,2048]{3,2,1,0:T(8,128)(2,1)} %param.12, bf16[1,1,2048,2048]{3,2,1,0:T(8,128)(2,1)} %param.11, bf16[512,2048]{1,0:T(8,128)(2,1)S(1)} %copy-done.1, f32[512]{0:T(512)S(1)} %add_rsqrt_fusion.3), kind=kOutput, calls=%fused_computation.45 | convolution fusion | flops 8603566080 | bytes 20973568 | tf_op jit(solution)/shard_map/dot_general | solution.py:45
  140.9 16.8 %fusion.31 = bf16[512,2048]{1,0:T(8,128)(2,1)} fusion(bf16[1,1,2048,2048]{3,2,1,0:T(8,128)(2,1)} %param.12, bf16[1,1,2048,2048]{3,2,1,0:T(8,128)(2,1)} %param.11, bf16[512,2048]{1,0:T(8,128)(2,1)} %all-gather.5.cloned.1.call-done, f32[512]{0:T(512)S(1)} %add_rsqrt_fusion.1), kind=kOutput, calls=%fused_computation.46 | convolution fusion | flops 8603566080 | bytes 20973568 | tf_op jit(solution)/shard_map/dot_general | solution.py:45
  157.7 0.0 all-reduce.5.cloned.1.call-update
  157.8 104.4 %all-reduce.5.cloned.1.call-done = (bf16[512,2048]{1,0:T(8,128)(2,1)}, bf16[512,2048]{1,0:T(8,128)(2,1)}) async-done(((bf16[512,2048]{1,0:T(8,128)(2,1)}, bf16[512,2048]{1,0:T(8,128)(2,1)}), (bf16[512,2048]{1,0:T(8,128)(2,1)}, bf16[512,2048]{1,0:T(8,128)(2,1)})) %all-reduce.5.cloned.1.call-update) | async-done | bytes 4194320 | tf_op jit(solution)/shard_map/psum | solution.py:46
  262.1 2.5 multiply_reduce_fusion.1
  264.7 0.3 copy-done.3
  265.0 0.8 multiply_reduce_fusion
  265.7 2.4 multiply_convert_fusion
  268.2 0.0 copy-done
  268.2 1.4 convolution_convert_fusion.1
  269.6 4.6 %all-to-all-start.1 = ((bf16[8,64,256]{2,1,0:T(8,128)(2,1)}), bf16[8,64,256]{2,1,0:T(8,128)(2,1)S(1)}, u32[]{:S(2)}, u32[]{:S(2)}) async-start(bf16[8,64,256]{2,1,0:T(8,128)(2,1)} %convolution_convert_fusion.1), calls=%async_computation.1 | async-start | bytes 524288 | tf_op jit(solution)/shard_map/all_to_all | solution.py:50
  274.2 1.4 convolution_convert_fusion
  275.6 8.3 %all-to-all-done.1 = bf16[8,64,256]{2,1,0:T(8,128)(2,1)S(1)} async-done(((bf16[8,64,256]{2,1,0:T(8,128)(2,1)}), bf16[8,64,256]{2,1,0:T(8,128)(2,1)S(1)}, u32[]{:S(2)}, u32[]{:S(2)}) %all-to-all-start.1) | async-done | bytes 262176 | tf_op jit(solution)/shard_map/all_to_all | solution.py:50
  284.0 3.4 %all-to-all-start.3 = ((bf16[8,64,256]{2,1,0:T(8,128)(2,1)}), bf16[8,64,256]{2,1,0:T(8,128)(2,1)S(1)}, u32[]{:S(2)}, u32[]{:S(2)}) async-start(bf16[8,64,256]{2,1,0:T(8,128)(2,1)} %convolution_convert_fusion), calls=%async_computation.3 | async-start | bytes 524288 | tf_op jit(solution)/shard_map/all_to_all | solution.py:50
  287.4 0.1 copy.17
  287.5 0.1 eq.54
  287.7 0.1 copy.21
  287.8 0.1 eq.65
  288.0 2.0 gather_fusion
  290.0 7.1 %all-to-all-done.3 = bf16[8,64,256]{2,1,0:T(8,128)(2,1)S(1)} async-done(((bf16[8,64,256]{2,1,0:T(8,128)(2,1)}), bf16[8,64,256]{2,1,0:T(8,128)(2,1)S(1)}, u32[]{:S(2)}, u32[]{:S(2)}) %all-to-all-start.3) | async-done | bytes 262176 | tf_op jit(solution)/shard_map/all_to_all | solution.py:50
  297.1 2.0 gather_fusion.2
  299.1 0.3 select_reduce_fusion.1
  299.4 8.9 %all-reduce.1 = (f32[256]{0:T(256)S(1)}, f32[256]{0:T(256)S(1)}) all-reduce(f32[256]{0:T(256)S(1)} %get-tuple-element.9, f32[256]{0:T(256)S(1)} %get-tuple-element.6), channel_id=1, replica_groups=mesh['section'=8,'mp'=4] {'mp'}, use_global_device_ids=true, to_apply=%region_20.21 | all-reduce | flops 512 | bytes 4096 | tf_op jit(solution)/shard_map/pmax | solution.py:58
  308.4 0.2 exponential_reduce_fusion.1
  308.5 0.2 exponential_reduce_fusion
  308.7 8.8 %all-reduce = (f32[256]{0:T(256)S(1)}, f32[256]{0:T(256)S(1)}, f32[256]{0:T(256)S(1)}, f32[256]{0:T(256)S(1)}) all-reduce(f32[256]{0:T(256)S(1)} %exponential_reduce_fusion, f32[256]{0:T(256)S(1)} %get-tuple-element.10, f32[256]{0:T(256)S(1)} %exponential_reduce_fusion.1, ...), channel_id=1, replica_groups=mesh['section'=8,'mp'=4] {'mp'}, use_global_device_ids=true, to_apply=%region_22.23 | all-reduce | flops 1024 | bytes 8192 | tf_op jit(solution)/shard_map/psum | solution.py:64
  317.5 0.1 stack_reshape.6
  317.7 0.1 copy.24
  317.7 0.2 stack_reshape.7
  317.9 0.1 copy.25
  318.0 0.6 pad_maximum_fusion
  (30 shorter events, 0.3 us)
Async XLA Ops:
  6.5 261.6 %copy-start = (bf16[1,2048,256]{2,1,0:T(8,128)(2,1)S(1)}, bf16[1,2048,256]{2,1,0:T(8,128)(2,1)}, u32[]{:S(2)}) copy-start(bf16[1,2048,256]{2,1,0:T(8,128)(2,1)} %param.13) | copy-start | bytes 3145732
  6.5 8.4 %copy-start.6 = (f32[128,2,512]{2,1,0:T(2,128)S(1)}, f32[128,2,512]{2,1,0:T(2,128)}, u32[]{:S(2)}) copy-start(f32[128,2,512]{2,1,0:T(2,128)} %param.9) | copy-start | bytes 1572868
  6.5 79.1 %all-gather.3.cloned.1.call-start = ((), (), s32[]{:S(2)}) async-start(), calls=%async_computation.4 | async-start | bytes 2621440 | tf_op jit(solution)/shard_map/all_gather | solution.py:39
  51.4 71.3 %all-gather.5.cloned.1.call-start = ((), (), s32[]{:S(2)}) async-start(), calls=%async_computation.5 | async-start | bytes 2621440 | tf_op jit(solution)/shard_map/all_gather | solution.py:39
  83.9 178.2 %all-reduce.5.cloned.1.call-start = ((), (), s32[]{:S(2)}) async-start(), calls=%async_computation.6 | async-start | bytes 8388608 | tf_op jit(solution)/shard_map/psum | solution.py:46
  85.7 39.1 %copy-start.1 = (bf16[512,2048]{1,0:T(8,128)(2,1)S(1)}, bf16[512,2048]{1,0:T(8,128)(2,1)}, u32[]{:S(2)}) copy-start(bf16[512,2048]{1,0:T(8,128)(2,1)} %all-gather.3.cloned.1.call-done) | copy-start | bytes 6291460
  262.1 2.5 copy-start.2
  262.1 2.9 copy-start.3
  262.1 3.6 %copy-start.4 = (bf16[512,2048]{1,0:T(8,128)(2,1)S(1)}, bf16[512,2048]{1,0:T(8,128)(2,1)}, u32[]{:S(2)}) copy-start(bf16[512,2048]{1,0:T(8,128)(2,1)} %get-tuple-element.18) | copy-start | bytes 6291460
  268.2 6.1 %copy-start.5 = (bf16[512,2048]{1,0:T(8,128)(2,1)S(1)}, bf16[512,2048]{1,0:T(8,128)(2,1)}, u32[]{:S(2)}) copy-start(bf16[512,2048]{1,0:T(8,128)(2,1)} %get-tuple-element.25) | copy-start | bytes 6291460
  268.2 19.2 %copy-start.7 = (s32[2,128,2]{1,2,0:T(2,128)S(1)}, s32[2,128,2]{1,2,0:T(2,128)}, u32[]{:S(2)}) copy-start(s32[2,128,2]{1,2,0:T(2,128)} %param.8) | copy-start | bytes 6148
  269.6 14.3 %all-to-all-start.1 = ((bf16[8,64,256]{2,1,0:T(8,128)(2,1)}), bf16[8,64,256]{2,1,0:T(8,128)(2,1)S(1)}, u32[]{:S(2)}, u32[]{:S(2)}) async-start(bf16[8,64,256]{2,1,0:T(8,128)(2,1)} %convolution_convert_fusion.1), calls=%async_computation.1 | async-start | bytes 524288 | tf_op jit(solution)/shard_map/all_to_all | solution.py:50
  284.0 13.1 %all-to-all-start.3 = ((bf16[8,64,256]{2,1,0:T(8,128)(2,1)}), bf16[8,64,256]{2,1,0:T(8,128)(2,1)S(1)}, u32[]{:S(2)}, u32[]{:S(2)}) async-start(bf16[8,64,256]{2,1,0:T(8,128)(2,1)} %convolution_convert_fusion), calls=%async_computation.3 | async-start | bytes 524288 | tf_op jit(solution)/shard_map/all_to_all | solution.py:50
Sparse Core Ops, SparseCore 0:
  51.6 34.0 all-gather.2
  87.5 35.1 all-gather.4
  157.9 104.1 all-reduce.4
where the time goes:
time: 326 us; the launch traced here: 325 us
  waiting for transfers between devices  156 us (48%)
  blocking collectives  57.7 us (18%)
  local copies, waits for them, and re-layouts  39.2 us (12%)
  matrix products  35.8 us (11%)
  other arithmetic  14.7 us (5%)
  between operations  13.3 us (4%)
  starting transfers between devices  8.28 us (3%)
    psum x1, waiting for transfers between devices, per_device(): lax.psum(partial_value.astype(jnp.bfloat16), 'mp').astype(jnp.float32)  104 us
    all_to_all x2, blocking collectives, per_device(): lax.all_to_all(outgoing, 'section', split_axis=0, concat_axis=0, tiled=True)  40 us
    all_gather x2, waiting for transfers between devices, per_device(): lax.all_gather(arrived.reshape(served, feat_width), 'mp', axis=1, tiled=T...  36.3 us
    dot_general x2, matrix products, per_device(): jnp.dot(hidden, w_out[0, 0], preferred_element_type=jnp.float32)  32.9 us
    scatter x2, local copies, waits for them, and re-layouts, per_device(): outgoing = jnp.zeros((sections, slot_cap, feat_width), jnp.bfloat16).at[o...  27.6 us
    all_to_all x2, waiting for transfers between devices, per_device(): lax.all_to_all(logits.reshape(sections, slot_cap, action_width).astype(jn...  15.4 us
    pmax x1, blocking collectives, per_device(): row_peak = lax.pmax(jnp.max(row_logits, axis=1), 'mp')  8.94 us
    psum x1, blocking collectives, per_device(): row_total, picked = lax.psum((local_total, local_pick), 'mp')  8.77 us
  transfers between devices with their start and end apart: 5, of which 5 were waited for; matrix products, arithmetic and copies ran while one was open for 6% of the time, Pallas kernels for 0%

commit v1 on v0

v1 whole, which is shorter than its diff:
```python
import functools

import jax
import jax.numpy as jnp
from jax import lax
from jax.experimental import pallas as pl
from jax.experimental.pallas import tpu as pltpu
from jax.sharding import PartitionSpec as P

STEPS = 2
META = 8
DIGIT = 32
VMEM = 48 * 1024 * 1024

norm_eps = 1e-06
f32 = jnp.float32
bf16 = jnp.bfloat16


def rms_round(source):
    widened = source.astype(f32)
    scale = lax.rsqrt(jnp.mean(widened * widened, axis=-1, keepdims=True) + norm_eps)
    return (widened * scale).astype(bf16)


def iota(shape, dim):
    return lax.broadcasted_iota(jnp.int32, shape, dim)


def nt_dot(left, right):
    return lax.dot_general(left, right, (((1,), (1,)), ((), ())), preferred_element_type=f32)


def slots_row(own_row, own_col):
    rows = own_row.shape[1]
    earlier = (own_col == own_row) & (iota((rows, rows), 0) < iota((rows, rows), 1))
    return jnp.sum(earlier.astype(jnp.int32), axis=0, keepdims=True)


def pack_kernel(sections, cap, own_row, own_col, meta, state, out):
    games, _, feat = state.shape
    rows = 2 * games
    dest = own_row[...] * cap + slots_row(own_row[...], own_col[...])
    select = (iota((sections * cap, rows), 0) == dest).astype(bf16)
    first = jnp.dot(select[:, :games], state[:, 0, :].astype(bf16), preferred_element_type=f32)
    second = jnp.dot(select[:, games:], state[:, 1, :].astype(bf16), preferred_element_type=f32)
    packed = (first + second).astype(bf16)
    notes = nt_dot(meta[...], select).astype(bf16)
    for s in range(sections):
        out[s, :cap, :] = packed[s * cap : (s + 1) * cap]
        out[s, cap:, :] = jnp.zeros((META, feat), bf16)
        out[s, cap:, :cap] = notes[:, s * cap : (s + 1) * cap]


def unpack_kernel(sections, cap, size, mp_ref, arrived, embed, x0_out, x1_out, notes_out, place_out):
    slots = sections * cap
    group = size // 4
    m = mp_ref[0]
    rows = jnp.concatenate([arrived[s, :cap, :] for s in range(sections)], axis=0)
    notes = jnp.concatenate([arrived[s, cap:, :cap] for s in range(sections)], axis=1)
    live = notes[META - 1 : META, :].astype(f32)
    before = (iota((slots, slots), 0) < iota((slots, slots), 1)).astype(bf16)
    rank = jnp.dot(jnp.broadcast_to(live, (8, slots)).astype(bf16), before, preferred_element_type=f32)
    rank = rank[:1].astype(jnp.int32)
    block = rank // group
    place = jnp.where(live > 0, (block ^ m) * group + (rank - block * group), -1)
    select = (iota((size, slots), 0) == place).astype(bf16)
    x0 = jnp.dot(select, rows, preferred_element_type=f32)
    mine = nt_dot(select, notes)
    own = (mine[:, 0:1] * DIGIT + mine[:, 1:2]).astype(jnp.int32)
    other = (mine[:, 2:3] * DIGIT + mine[:, 3:4]).astype(jnp.int32)
    columns = iota((size, embed.shape[0]), 1)
    effect = jnp.where(columns == own, 1.0, 0.0) + jnp.where(columns == other, 0.5, 0.0)
    moved = jnp.dot(effect.astype(bf16), embed[...], preferred_element_type=f32)
    x0_out[...] = x0.astype(bf16)
    x1_out[...] = (0.8 * x0 + moved).astype(bf16)
    notes_out[...] = mine[: size // 4]
    place_out[...] = place


def serve_kernel(size, tiles, mp_ref, own, px, py, da, db, w_in, w_out, send_a, send_b, keep_a, keep_b, mine, x_full, hidden, scale):
    feat = own.shape[1]
    group = size // 4
    width = w_in.shape[1]
    half = x_full.shape[1] // 2
    m = mp_ref[0]
    step = pl.program_id(0)

    @pl.when(step == 0)
    def _():
        total = jnp.zeros((size, 1), f32)
        for k in range(4):
            parts = []
            for j in range(4):
                b = j ^ k
                if k == 3:
                    src = da if b < 2 else db
                    parts.append(src[(b % 2) * group : (b % 2 + 1) * group, :])
                else:
                    src = (own, px, py)[k]
                    parts.append(src[b * group : (b + 1) * group, :])
            chunk = jnp.concatenate(parts, axis=0)
            x_full[:, pl.ds(pl.multiple_of((m ^ k) * feat, feat), feat)] = chunk
            wide = chunk.astype(f32)
            total = total + jnp.sum(wide * wide, axis=1, keepdims=True)
        scale[...] = lax.rsqrt(total / (4 * feat) + norm_eps)
        mine[...] = x_full[:group, :]

    for t in range(tiles):

        @pl.when(step == t)
        def _():
            z = jnp.dot(x_full[...], w_in[...], preferred_element_type=f32)
            hidden[:, t * width : (t + 1) * width] = jax.nn.gelu(z * scale[...]).astype(bf16)

    for t in range(tiles):

        @pl.when(step == tiles + t)
        def _():
            part = jnp.dot(hidden[...], w_out[...], preferred_element_type=f32).astype(bf16)
            g = [part[j * group : (j + 1) * group] for j in range(4)]
            if t < tiles // 2:
                cols = slice(t * width, (t + 1) * width)
                send_a[:group, cols] = g[1]
                send_a[group:, cols] = g[3]
                keep_a[:group, cols] = g[0]
                keep_a[group:, cols] = g[2]
            else:
                cols = slice(t * width - half, (t + 1) * width - half)
                send_b[:group, cols] = g[2]
                send_b[group:, cols] = g[3]
                keep_b[:group, cols] = g[0]
                keep_b[group:, cols] = g[1]


def fold_kernel(keep_a, got_a, keep_b, got_b, out_a, out_b):
    out_a[...] = (keep_a[...].astype(f32) + got_a[...].astype(f32)).astype(bf16)
    out_b[...] = (keep_b[...].astype(f32) + got_b[...].astype(f32)).astype(bf16)


def score_kernel(sections, cap, step_idx, mp_ref, mine, keep_a, got_a, last_a, keep_b, got_b, last_b, h0, h1, h2, h3a, h3b, notes, place, out):
    group, width = mine.shape
    half = width // 2
    m = mp_ref[0]
    wide = lambda ref: ref[...].astype(f32)
    sum_a = keep_a[:group].astype(f32) + got_a[:group].astype(f32) + wide(last_a)
    sum_b = keep_b[:group].astype(f32) + got_b[:group].astype(f32) + wide(last_b)
    x = wide(mine)
    ha = x[:, :half] + sum_a
    hb = x[:, half:] + sum_b
    square = jnp.sum(ha * ha, axis=1, keepdims=True) + jnp.sum(hb * hb, axis=1, keepdims=True)
    scale = lax.rsqrt(square / width + norm_eps)
    na = (ha * scale).astype(bf16)
    nb = (hb * scale).astype(bf16)
    c = 4 * step_idx
    chosen = (notes[:, c : c + 1] * DIGIT + notes[:, c + 1 : c + 2]).astype(jnp.int32)
    logits = []
    for k in range(4):
        top, bottom = (h3a[...], h3b[...]) if k == 3 else ((h0, h1, h2)[k][:half], (h0, h1, h2)[k][half:])
        logits.append(
            jnp.dot(na, top, preferred_element_type=f32) + jnp.dot(nb, bottom, preferred_element_type=f32)
        )
    peak = functools.reduce(jnp.maximum, [jnp.max(v, axis=1, keepdims=True) for v in logits])
    total = jnp.zeros((group, 1), f32)
    picked = jnp.zeros((group, 1), f32)
    for k, v in enumerate(logits):
        columns = iota(v.shape, 1) + (m ^ k) * v.shape[1]
        total = total + jnp.sum(jnp.exp(v - peak), axis=1, keepdims=True)
        picked = picked + jnp.sum(jnp.where(columns == chosen, v, 0.0), axis=1, keepdims=True)
    logp = picked - peak - jnp.log(total)
    slots = sections * cap
    spread = jnp.where(iota((group, slots), 0) == place[...], logp, 0.0)
    spread = jnp.sum(spread, axis=0, keepdims=True)
    for s in range(sections):
        out[s : s + 1, :] = spread[:, s * cap : (s + 1) * cap]


def return_kernel(sections, cap, own_row, own_col, got, out):
    rows = own_row.shape[1]
    dest = own_row[...] * cap + slots_row(own_row[...], own_col[...])
    pick = iota((sections * cap, rows), 0) == dest
    for t in range(STEPS):
        column = got[:, t : t + 1]
        out[t : t + 1, :] = jnp.sum(jnp.where(pick, column, 0.0), axis=0, keepdims=True)


def call(kernel, outs, cost=None, **kw):
    return pl.pallas_call(
        kernel,
        out_shape=outs,
        compiler_params=pltpu.CompilerParams(vmem_limit_bytes=VMEM),
        cost_estimate=cost,
        **kw,
    )


def shape(*dims, dtype=bf16):
    return jax.ShapeDtypeStruct(dims, dtype)


SMEM_SPEC = pl.BlockSpec(memory_space=pltpu.SMEM)
VMEM_SPEC = pl.BlockSpec(memory_space=pltpu.VMEM)


def plane_plan(matches, actions, state, embed, w_in, w_out, head):
    sections = lax.axis_size("section")
    games, _, feat = state.shape
    cap = 4 * games // sections
    rows = 2 * games
    slots = sections * cap
    width = 4 * feat
    m = lax.axis_index("mp").astype(jnp.int32).reshape(1)
    over_x = lambda v: lax.ppermute(v, "mp", [(i, i ^ 1) for i in range(4)])
    over_y = lambda v: lax.ppermute(v, "mp", [(i, i ^ 2) for i in range(4)])

    def gather(v):
        h = v.shape[0] // 2
        from_x, from_y = over_x(v), over_y(v)
        return from_x, from_y, over_y(from_x[:h]), over_x(from_y[h:])

    own_row = matches.T.reshape(1, rows)
    own_col = own_row.reshape(rows, 1)
    acts = actions.transpose(0, 2, 1)
    mine0, other0, mine1 = acts[0].reshape(rows), acts[0, ::-1].reshape(rows), acts[1].reshape(rows)
    notes = jnp.stack(
        [
            mine0 // DIGIT, mine0 % DIGIT, other0 // DIGIT, other0 % DIGIT,
            mine1 // DIGIT, mine1 % DIGIT, jnp.zeros_like(mine0), jnp.ones_like(mine0),
        ]
    ).astype(bf16)

    head_own = head[0]
    heads = (head_own,) + gather(head_own)

    packed = call(functools.partial(pack_kernel, sections, cap), shape(sections, cap + META, feat))(
        own_row, own_col, notes, state
    )
    arrived = lax.all_to_all(packed, "section", split_axis=0, concat_axis=0, tiled=True)
    size = slots
    group = size // 4
    x0, x1, notes_c, place = call(
        functools.partial(unpack_kernel, sections, cap, size),
        (shape(size, feat), shape(size, feat), shape(group, META, dtype=f32), shape(1, slots, dtype=jnp.int32)),
        in_specs=[SMEM_SPEC, VMEM_SPEC, VMEM_SPEC],
    )(m, arrived, embed)

    tiles = 4
    tile = w_in.shape[3] // tiles
    full = lambda r, c: pl.BlockSpec((r, c), lambda i: (0, 0))
    outs = []
    for step_idx, x in enumerate((x0, x1)):
        got = gather(x)
        send_a, send_b, keep_a, keep_b, mine = call(
            functools.partial(serve_kernel, size, tiles),
            (shape(size // 2, width // 2),) * 4 + (shape(group, width),),
            cost=pl.CostEstimate(flops=4 * size * width * w_in.shape[3], bytes_accessed=4 * width * w_in.shape[3], transcendentals=0),
            grid=(2 * tiles,),
            in_specs=[
                SMEM_SPEC,
                full(size, feat), full(size, feat), full(size, feat), full(size // 2, feat), full(size // 2, feat),
                pl.BlockSpec((w_in.shape[2], tile), lambda i: (0, jnp.minimum(i, tiles - 1))),
                pl.BlockSpec((w_out.shape[2], width // tiles), lambda i: (0, jnp.maximum(i - tiles, 0))),
            ],
            out_specs=tuple([full(size // 2, width // 2)] * 4 + [full(group, width)]),
            scratch_shapes=[
                pltpu.VMEM((size, width), bf16),
                pltpu.VMEM((size, w_in.shape[3]), bf16),
                pltpu.VMEM((size, 1), f32),
            ],
        )(m, x, *got, w_in[0, 0], w_out[0, 0])
        got_a, got_b = over_x(send_a), over_y(send_b)
        second = pl.BlockSpec((group, width // 2), lambda i: (1, 0))
        fold_a, fold_b = call(
            fold_kernel,
            (shape(group, width // 2),) * 2,
            grid=(1,),
            in_specs=[second] * 4,
            out_specs=(full(group, width // 2),) * 2,
        )(keep_a, got_a, keep_b, got_b)
        last_a, last_b = over_y(fold_a), over_x(fold_b)
        outs.append(
            call(
                functools.partial(score_kernel, sections, cap, step_idx),
                shape(sections, cap, dtype=f32),
                in_specs=[SMEM_SPEC] + [VMEM_SPEC] * 14,
            )(m, mine, keep_a, got_a, last_a, keep_b, got_b, last_b, *heads, notes_c, place)
        )
    sent = jnp.concatenate(outs, axis=1)
    sent = jnp.broadcast_to(sent[:, None], (sections, 4, STEPS * cap)).reshape(sections * 4, STEPS * cap)
    back = lax.all_to_all(sent, ("section", "mp"), split_axis=0, concat_axis=0, tiled=True)
    back = back.reshape(sections, 4, STEPS, cap).sum(axis=1)
    back = back.transpose(0, 2, 1).reshape(slots, STEPS)
    logp = call(functools.partial(return_kernel, sections, cap), shape(STEPS, rows, dtype=f32))(own_row, own_col, back)
    return logp.reshape(STEPS, 2, games).transpose(0, 2, 1)


def general_plan(matches, actions, state, embed, w_in, w_out, head):
    sections = lax.axis_size("section")
    game_count = matches.shape[0]
    feat_width = state.shape[2]
    slot_cap = 4 * game_count // sections
    served = sections * slot_cap
    owners = matches.reshape(-1)
    onehot = (owners[:, None] == jnp.arange(sections, dtype=jnp.int32)[None, :]).astype(jnp.int32)
    slot_of = jnp.sum((jnp.cumsum(onehot, axis=0) - onehot) * onehot, axis=1)
    action_width = head.shape[2]
    columns = lax.axis_index("mp") * action_width + jnp.arange(action_width, dtype=jnp.int32)
    current = state
    results = []
    for step_idx in range(STEPS):
        observed = current.astype(bf16).reshape(2 * game_count, feat_width)
        outgoing = jnp.zeros((sections, slot_cap, feat_width), bf16).at[owners, slot_of].set(observed)
        arrived = lax.all_to_all(outgoing, "section", split_axis=0, concat_axis=0, tiled=True)
        inputs = lax.all_gather(arrived.reshape(served, feat_width), "mp", axis=1, tiled=True)
        normed = rms_round(inputs)
        hidden = jax.nn.gelu(jnp.dot(normed, w_in[0, 0], preferred_element_type=f32)).astype(bf16)
        partial_value = jnp.dot(hidden, w_out[0, 0], preferred_element_type=f32)
        summed = inputs.astype(f32) + lax.psum(partial_value.astype(bf16), "mp").astype(f32)
        logits = jnp.dot(rms_round(summed), head[0], preferred_element_type=f32)
        returned = lax.all_to_all(
            logits.reshape(sections, slot_cap, action_width).astype(bf16),
            "section",
            split_axis=0,
            concat_axis=0,
            tiled=True,
        ).astype(f32)
        row_logits = returned[owners, slot_of]
        row_peak = lax.pmax(jnp.max(row_logits, axis=1), "mp")
        chosen = actions[step_idx].reshape(-1)
        local_total = jnp.sum(jnp.exp(row_logits - row_peak[:, None]), axis=1)
        local_pick = jnp.sum(jnp.where(columns[None, :] == chosen[:, None], row_logits, 0.0), axis=1)
        row_total, picked = lax.psum((local_total, local_pick), "mp")
        results.append((picked - row_peak - jnp.log(row_total)).reshape(game_count, 2))
        picked_rows = jnp.take(embed, actions[step_idx], axis=0).astype(f32)
        current = 0.8 * current + picked_rows + 0.5 * picked_rows[:, ::-1, :]
    return jnp.stack(results)


def solution(mesh):
    return jax.shard_map(
        plane_plan if mesh.shape["mp"] == 4 else general_plan,
        mesh=mesh,
        in_specs=(
            P("section", None),
            P(None, "section", None),
            P("section", None, "mp"),
            P(None, "mp"),
            P("section", None, None, "mp"),
            P("section", None, "mp", None),
            P("section", None, "mp"),
        ),
        out_specs=P(None, "section", None),
        check_vma=False,
    )
```

time: 326 us -> 158 us (0.48)
  waiting for transfers between devices: 156 us -> 72.6 us
  blocking collectives: 57.7 us -> 10.3 us
  Pallas kernels: 0 us -> 38.8 us
  matrix products: 35.8 us -> 0 us
  local copies, waits for them, and re-layouts: 39.2 us -> 6.02 us
  starting transfers between devices: 8.28 us -> 28.8 us
  other arithmetic: 14.7 us -> 0.85 us
  between operations: 13.3 us -> 0.21 us
    psum x1 -> x0, waiting for transfers between devices: 104 us -> none  [per_device(): lax.psum(partial_value.astype(jnp.bfloat16), 'mp').astype(jnp.float32)]
    ppermute x0 -> x20, waiting for transfers between devices: none -> 55.8 us  [the longest x10 28.2 us: plane_plan(): over_x = lambda v: lax.ppermute(v, 'mp', [(i, i ^ 1) for i in range(4)])]
    pallas_call x0 -> x9, Pallas kernels: none -> 38.8 us  [the longest x2 29 us: plane_plan(): call(functools.partial(serve_kernel, size, tiles), (shape(size // 2, widt...]
    all_gather x2 -> x0, waiting for transfers between devices: 36.3 us -> none  [per_device(): lax.all_gather(arrived.reshape(served, feat_width), 'mp', axis=1, tiled=T...]
    dot_general x4 -> x0, matrix products: 35.8 us -> none  [the longest x2 32.9 us: per_device(): jnp.dot(hidden, w_out[0, 0], preferred_element_type=jnp.float32)]
    all_to_all x2 -> x1, blocking collectives: 40 us -> 10.3 us  [plane_plan(): lax.all_to_all(sent, ('section', 'mp'), split_axis=0, concat_axis=0, tile...]
    scatter x2 -> x0, local copies, waits for them, and re-layouts: 27.6 us -> none  [per_device(): outgoing = jnp.zeros((sections, slot_cap, feat_width), jnp.bfloat16).at[o...]
    ppermute x0 -> x20, starting transfers between devices: none -> 22.4 us  [the longest x10 12 us: plane_plan(): over_y = lambda v: lax.ppermute(v, 'mp', [(i, i ^ 2) for i in range(4)])]
  transfers between devices with their start and end apart: 5 -> 21, of which waited for: 5 -> 8; matrix products, arithmetic and copies ran while one was open for 6% -> 0% of each run, Pallas kernels for 0% -> 20%
where the time goes in v1:
time: 158 us; the launch traced here: 157 us
  waiting for transfers between devices  72.6 us (46%)
  Pallas kernels  38.8 us (25%)
  starting transfers between devices  28.8 us (18%)
  blocking collectives  10.3 us (7%)
  local copies, waits for them, and re-layouts  6.02 us (4%)
    pallas_call x2, Pallas kernels, plane_plan(): call(functools.partial(serve_kernel, size, tiles), (shape(size // 2, widt...  29 us
    ppermute x10, waiting for transfers between devices, plane_plan(): over_x = lambda v: lax.ppermute(v, 'mp', [(i, i ^ 1) for i in range(4)])  28.2 us
    ppermute x10, waiting for transfers between devices, plane_plan(): over_y = lambda v: lax.ppermute(v, 'mp', [(i, i ^ 2) for i in range(4)])  27.6 us
    all_to_all x1, waiting for transfers between devices, plane_plan(): lax.all_to_all(packed, 'section', split_axis=0, concat_axis=0, tiled=True)  16.8 us
    ppermute x10, starting transfers between devices, plane_plan(): over_y = lambda v: lax.ppermute(v, 'mp', [(i, i ^ 2) for i in range(4)])  12 us
    ppermute x10, starting transfers between devices, plane_plan(): over_x = lambda v: lax.ppermute(v, 'mp', [(i, i ^ 1) for i in range(4)])  10.5 us
    all_to_all x1, blocking collectives, plane_plan(): lax.all_to_all(sent, ('section', 'mp'), split_axis=0, concat_axis=0, tile...  10.3 us
    all_to_all x1, starting transfers between devices, plane_plan(): lax.all_to_all(packed, 'section', split_axis=0, concat_axis=0, tiled=True)  6.32 us
  transfers between devices with their start and end apart: 21, of which 8 were waited for; matrix products, arithmetic and copies ran while one was open for 0% of the time, Pallas kernels for 20%

profile of v1, /device:TPU:0, one launch (start us, length us, event | category | flops | bytes accessed | tf_op | source)
XLA Modules:
  0.0 157.5 jit_solution(7030734458475317671)
XLA Ops:
  0.0 0.7 fusion.6
  0.8 0.8 copy.14.own_col
  1.7 0.0 copy-start.2
  1.7 1.0 copy-done.2
  2.7 0.7 copy-done.3
  3.4 1.8 %shard_map.73 = bf16[8,72,512]{2,1,0:T(8,128)(2,1)} custom-call(s32[1,256]{1,0:T(1,128)S(1)} %bitcast.23, s32[256,1]{1,0:T(8,128)S(1)} %copy.14.own_col, bf16[8,256]{1,0:T(8,128)(2,1)S(1)} %stack.3.meta, f32[128,2,512]{2,1,0:T(2,128)S(1)} %copy-done.2), custom_call_target="tpu_custom_call" | custom-call | tf_op jit(solution)/shard_map/pallas_call | solution.py:235
  5.2 6.3 %all-to-all-start = ((bf16[8,72,512]{2,1,0:T(8,128)(2,1)}), bf16[8,72,512]{2,1,0:T(8,128)(2,1)S(1)}, u32[]{:S(2)}, u32[]{:S(2)}) async-start(bf16[8,72,512]{2,1,0:T(8,128)(2,1)} %shard_map.73), calls=%async_computation | async-start | bytes 1179648 | tf_op jit(solution)/shard_map/all_to_all | solution.py:238
  11.6 16.8 %all-to-all-done.arrived = bf16[8,72,512]{2,1,0:T(8,128)(2,1)S(1)} async-done(((bf16[8,72,512]{2,1,0:T(8,128)(2,1)}), bf16[8,72,512]{2,1,0:T(8,128)(2,1)S(1)}, u32[]{:S(2)}, u32[]{:S(2)}) %all-to-all-start) | async-done | bytes 589856 | tf_op jit(solution)/shard_map/all_to_all | solution.py:238
  28.3 1.2 copy-done.1
  29.6 1.6 shard_map.74
  31.1 1.6 collective-permute-start
  32.7 1.5 collective-permute-start.1
  34.2 0.5 collective-permute-start.12
  34.7 0.5 collective-permute-start.13
  35.3 10.8 %collective-permute-done.px = bf16[512,512]{1,0:T(8,128)(2,1)S(1)} collective-permute-done((bf16[512,512]{1,0:T(8,128)(2,1)S(1)}, bf16[512,512]{1,0:T(8,128)(2,1)S(1)}, u32[]{:S(2)}, u32[]{:S(2)}) %collective-permute-start) | collective-permute-done | bytes 524320 | tf_op jit(solution)/shard_map/ppermute | solution.py:213
  46.1 1.6 %collective-permute-start.2 = (bf16[256,512]{1,0:T(8,128)(2,1)S(1)}, bf16[256,512]{1,0:T(8,128)(2,1)S(1)}, u32[]{:S(2)}, u32[]{:S(2)}) collective-permute-start(bf16[256,512]{1,0:T(8,128)(2,1)S(1)} %slice.35), channel_id=1, source_target_pairs={{0,2},{1,3},{2,0},{3,1},{4,6},{5,7},{6,4},{7,5},{8,10},{9,11},{10,... | collective-permute-start | bytes 786440 | tf_op jit(solution)/shard_map/ppermute | solution.py:214
  47.6 0.0 collective-permute-done.1.py
  47.7 1.6 collective-permute-start.3
  49.2 0.5 collective-permute-start.8
  49.8 7.5 %collective-permute-done.12.px = bf16[512,512]{1,0:T(8,128)(2,1)S(1)} collective-permute-done((bf16[512,512]{1,0:T(8,128)(2,1)S(1)}, bf16[512,512]{1,0:T(8,128)(2,1)S(1)}, u32[]{:S(2)}, u32[]{:S(2)}) %collective-permute-start.12) | collective-permute-done | bytes 524320 | tf_op jit(solution)/shard_map/ppermute | solution.py:213
  57.3 1.5 collective-permute-start.9
  58.8 0.0 collective-permute-done.13.py
  58.8 1.5 collective-permute-start.14
  60.3 4.1 %collective-permute-done.2.da = bf16[256,512]{1,0:T(8,128)(2,1)S(1)} collective-permute-done((bf16[256,512]{1,0:T(8,128)(2,1)S(1)}, bf16[256,512]{1,0:T(8,128)(2,1)S(1)}, u32[]{:S(2)}, u32[]{:S(2)}) %collective-permute-start.2) | collective-permute-done | bytes 262176 | tf_op jit(solution)/shard_map/ppermute | solution.py:214
  64.4 0.5 collective-permute-start.15
  64.9 0.0 collective-permute-done.3.db
  64.9 14.5 %shard_map.75 = (bf16[256,1024]{1,0:T(8,128)(2,1)S(1)}, bf16[256,1024]{1,0:T(8,128)(2,1)S(1)}, bf16[256,1024]{1,0:T(8,128)(2,1)S(1)}, bf16[256,1024]{1,0:T(8,128)(2,1)S(1)}, bf16[128,2048]{1,0:T(8,128)(2,1)S(1)}) custom-call(s32[1]{0:T(128)} %bitcast.3.mp_ref, bf16[512,512]{1,0:T(8,128)(2,1)S(1)} %get-tuple-element.23.own, ...), custom_call_target="tpu_custom_call" | custom-call | flops 8589934592 | bytes 16777216 | tf_op jit(solution)/shard_map/pallas_call | solution.py:253
  79.4 1.6 collective-permute-start.4
  81.0 9.8 %collective-permute-done.14.da = bf16[256,512]{1,0:T(8,128)(2,1)S(1)} collective-permute-done((bf16[256,512]{1,0:T(8,128)(2,1)S(1)}, bf16[256,512]{1,0:T(8,128)(2,1)S(1)}, u32[]{:S(2)}, u32[]{:S(2)}) %collective-permute-start.14) | collective-permute-done | bytes 262176 | tf_op jit(solution)/shard_map/ppermute | solution.py:214
  90.8 1.5 collective-permute-start.5
  92.3 0.0 collective-permute-done.15.db
  92.3 14.5 %shard_map.78 = (bf16[256,1024]{1,0:T(8,128)(2,1)S(1)}, bf16[256,1024]{1,0:T(8,128)(2,1)S(1)}, bf16[256,1024]{1,0:T(8,128)(2,1)S(1)}, bf16[256,1024]{1,0:T(8,128)(2,1)S(1)}, bf16[128,2048]{1,0:T(8,128)(2,1)S(1)}) custom-call(s32[1]{0:T(128)} %bitcast.3.mp_ref, bf16[512,512]{1,0:T(8,128)(2,1)S(1)} %get-tuple-element.33.own, ...), custom_call_target="tpu_custom_call" | custom-call | flops 8589934592 | bytes 16777216 | tf_op jit(solution)/shard_map/pallas_call | solution.py:253
  106.8 0.6 collective-permute-start.16
  107.5 0.0 collective-permute-done.8.h1
  107.5 1.1 collective-permute-start.17
  108.6 0.0 collective-permute-done.9.h2
  108.6 1.0 collective-permute-start.10
  109.6 0.0 collective-permute-done.4.got_a
  109.7 1.6 collective-permute-start.11
  111.2 0.0 collective-permute-done.5.got_b
  111.2 0.1 shard_map.76
  111.3 0.6 collective-permute-start.6
  111.9 9.9 %collective-permute-done.16.got_a = bf16[256,1024]{1,0:T(8,128)(2,1)S(1)} collective-permute-done((bf16[256,1024]{1,0:T(8,128)(2,1)S(1)}, bf16[256,1024]{1,0:T(8,128)(2,1)S(1)}, u32[]{:S(2)}, u32[]{:S(2)}) %collective-permute-start.16) | collective-permute-done | bytes 524320 | tf_op jit(solution)/shard_map/ppermute | solution.py:213
  121.8 0.5 collective-permute-start.7
  122.3 0.0 collective-permute-done.17.got_b
  122.3 0.1 shard_map.79
  122.4 1.2 collective-permute-start.18
  123.6 9.9 %collective-permute-done.10.h3a = bf16[1024,256]{1,0:T(8,128)(2,1)S(1)} collective-permute-done((bf16[1024,256]{1,0:T(8,128)(2,1)S(1)}, bf16[1024,256]{1,0:T(8,128)(2,1)S(1)}, u32[]{:S(2)}, u32[]{:S(2)}) %collective-permute-start.10) | collective-permute-done | bytes 524320 | tf_op jit(solution)/shard_map/ppermute | solution.py:214
  133.6 1.5 collective-permute-start.19
  135.0 0.0 collective-permute-done.11.h3b
  135.0 3.8 %collective-permute-done.6.last_a = bf16[128,1024]{1,0:T(8,128)(2,1)S(1)} collective-permute-done((bf16[128,1024]{1,0:T(8,128)(2,1)S(1)}, bf16[128,1024]{1,0:T(8,128)(2,1)S(1)}, u32[]{:S(2)}, u32[]{:S(2)}) %collective-permute-start.6) | collective-permute-done | bytes 262176 | tf_op jit(solution)/shard_map/ppermute | solution.py:214
  138.8 0.0 collective-permute-done.7.last_b
  138.8 2.9 %shard_map.77 = f32[8,64]{1,0:T(8,128)S(1)} custom-call(s32[1]{0:T(128)} %bitcast.3.mp_ref, bf16[128,2048]{1,0:T(8,128)(2,1)S(1)} %get-tuple-element.24.mine, bf16[256,1024]{1,0:T(8,128)(2,1)S(1)} %get-tuple-element.25.keep_a, bf16[256,1024]{1,0:T(8,128)(2,1)S(1)} %collective-permute-done.4.got_a, bf16[128,1024]{1,0:T(8,128)(2,1)S(1)} %collective-permute-done.6.last_a, ...), custom_call_target="tpu_custom_call" | custom-call | tf_op jit(solution)/shard_map/pallas_call | solution.py:282
  141.8 0.0 collective-permute-done.18.last_a
  141.8 0.0 collective-permute-done.19.last_b
  141.8 2.9 %shard_map.80 = f32[8,64]{1,0:T(8,128)S(1)} custom-call(s32[1]{0:T(128)} %bitcast.3.mp_ref, bf16[128,2048]{1,0:T(8,128)(2,1)S(1)} %get-tuple-element.34.mine, bf16[256,1024]{1,0:T(8,128)(2,1)S(1)} %get-tuple-element.35.keep_a, bf16[256,1024]{1,0:T(8,128)(2,1)S(1)} %collective-permute-done.16.got_a, bf16[128,1024]{1,0:T(8,128)(2,1)S(1)} %collective-permute-done.18.last_a, ...), custom_call_target="tpu_custom_call" | custom-call | tf_op jit(solution)/shard_map/pallas_call | solution.py:282
  144.7 0.1 pad_maximum_fusion
  144.8 10.3 %all_to_all.14 = f32[32,1,128]{2,1,0:T(1,128)S(1)} all-to-all(f32[32,1,128]{2,1,0:T(1,128)S(1)} %bitcast.25), channel_id=1, replica_groups=mesh['section'=8,'mp'=4] {'section','mp'}, dimensions={0} | all-to-all | bytes 32768 | tf_op jit(solution)/shard_map/all_to_all | solution.py:290
  155.1 0.5 broadcast.282
  155.6 0.7 reduce.3
  156.3 0.1 reshape.329
  156.4 0.1 copy.13
  156.6 0.3 shard_map.81
  156.9 0.6 reshape.331
  (27 shorter events, 0.3 us)
Async XLA Ops:
  1.7 1.0 copy-start.2
  2.7 0.7 copy-start.3
  5.2 23.1 %all-to-all-start = ((bf16[8,72,512]{2,1,0:T(8,128)(2,1)}), bf16[8,72,512]{2,1,0:T(8,128)(2,1)S(1)}, u32[]{:S(2)}, u32[]{:S(2)}) async-start(bf16[8,72,512]{2,1,0:T(8,128)(2,1)} %shard_map.73), calls=%async_computation | async-start | bytes 1179648 | tf_op jit(solution)/shard_map/all_to_all | solution.py:238
  28.3 1.2 copy-start.1
  31.1 14.9 %collective-permute-start = (bf16[512,512]{1,0:T(8,128)(2,1)S(1)}, bf16[512,512]{1,0:T(8,128)(2,1)S(1)}, u32[]{:S(2)}, u32[]{:S(2)}) collective-permute-start(bf16[512,512]{1,0:T(8,128)(2,1)S(1)} %get-tuple-element.23.own), channel_id=1, source_target_pairs={{0,1},{1,0},{2,3},{3,2},{4,5},{5,4},{6,7},{7,6},{8,9},{9,8},{10,11... | collective-permute-start | bytes 1572872 | tf_op jit(solution)/shard_map/ppermute | solution.py:213
  32.7 15.0 %collective-permute-start.1 = (bf16[512,512]{1,0:T(8,128)(2,1)S(1)}, bf16[512,512]{1,0:T(8,128)(2,1)S(1)}, u32[]{:S(2)}, u32[]{:S(2)}) collective-permute-start(bf16[512,512]{1,0:T(8,128)(2,1)S(1)} %get-tuple-element.23.own), channel_id=1, source_target_pairs={{0,2},{1,3},{2,0},{3,1},{4,6},{5,7},{6,4},{7,5},{8,10},{9,11},{10,... | collective-permute-start | bytes 1572872 | tf_op jit(solution)/shard_map/ppermute | solution.py:214
  34.2 23.1 %collective-permute-start.12 = (bf16[512,512]{1,0:T(8,128)(2,1)S(1)}, bf16[512,512]{1,0:T(8,128)(2,1)S(1)}, u32[]{:S(2)}, u32[]{:S(2)}) collective-permute-start(bf16[512,512]{1,0:T(8,128)(2,1)S(1)} %get-tuple-element.33.own), channel_id=1, source_target_pairs={{0,1},{1,0},{2,3},{3,2},{4,5},{5,4},{6,7},{7,6},{8,9},{9,8},{10,11... | collective-permute-start | bytes 1572872 | tf_op jit(solution)/shard_map/ppermute | solution.py:213
  34.7 24.1 %collective-permute-start.13 = (bf16[512,512]{1,0:T(8,128)(2,1)S(1)}, bf16[512,512]{1,0:T(8,128)(2,1)S(1)}, u32[]{:S(2)}, u32[]{:S(2)}) collective-permute-start(bf16[512,512]{1,0:T(8,128)(2,1)S(1)} %get-tuple-element.33.own), channel_id=1, source_target_pairs={{0,2},{1,3},{2,0},{3,1},{4,6},{5,7},{6,4},{7,5},{8,10},{9,11},{10,... | collective-permute-start | bytes 1572872 | tf_op jit(solution)/shard_map/ppermute | solution.py:214
  46.1 18.3 %collective-permute-start.2 = (bf16[256,512]{1,0:T(8,128)(2,1)S(1)}, bf16[256,512]{1,0:T(8,128)(2,1)S(1)}, u32[]{:S(2)}, u32[]{:S(2)}) collective-permute-start(bf16[256,512]{1,0:T(8,128)(2,1)S(1)} %slice.35), channel_id=1, source_target_pairs={{0,2},{1,3},{2,0},{3,1},{4,6},{5,7},{6,4},{7,5},{8,10},{9,11},{10,... | collective-permute-start | bytes 786440 | tf_op jit(solution)/shard_map/ppermute | solution.py:214
  47.7 17.3 %collective-permute-start.3 = (bf16[256,512]{1,0:T(8,128)(2,1)S(1)}, bf16[256,512]{1,0:T(8,128)(2,1)S(1)}, u32[]{:S(2)}, u32[]{:S(2)}) collective-permute-start(bf16[256,512]{1,0:T(8,128)(2,1)S(1)} %slice.36), channel_id=1, source_target_pairs={{0,1},{1,0},{2,3},{3,2},{4,5},{5,4},{6,7},{7,6},{8,9},{9,8},{10,11... | collective-permute-start | bytes 786440 | tf_op jit(solution)/shard_map/ppermute | solution.py:213
  49.2 58.2 %collective-permute-start.8 = (bf16[2048,256]{1,0:T(8,128)(2,1)}, bf16[2048,256]{1,0:T(8,128)(2,1)S(1)}, u32[]{:S(2)}, u32[]{:S(2)}) collective-permute-start(bf16[2048,256]{1,0:T(8,128)(2,1)} %bitcast.17), channel_id=1, source_target_pairs={{0,1},{1,0},{2,3},{3,2},{4,5},{5,4},{6,7},{7,6},{8,9},{9,8},{10,11... | collective-permute-start | bytes 3145736 | tf_op jit(solution)/shard_map/ppermute | solution.py:213
  57.3 51.3 %collective-permute-start.9 = (bf16[2048,256]{1,0:T(8,128)(2,1)}, bf16[2048,256]{1,0:T(8,128)(2,1)S(1)}, u32[]{:S(2)}, u32[]{:S(2)}) collective-permute-start(bf16[2048,256]{1,0:T(8,128)(2,1)} %bitcast.18), channel_id=1, source_target_pairs={{0,2},{1,3},{2,0},{3,1},{4,6},{5,7},{6,4},{7,5},{8,10},{9,11},{10,... | collective-permute-start | bytes 3145736 | tf_op jit(solution)/shard_map/ppermute | solution.py:214
  58.8 32.0 %collective-permute-start.14 = (bf16[256,512]{1,0:T(8,128)(2,1)S(1)}, bf16[256,512]{1,0:T(8,128)(2,1)S(1)}, u32[]{:S(2)}, u32[]{:S(2)}) collective-permute-start(bf16[256,512]{1,0:T(8,128)(2,1)S(1)} %slice.39), channel_id=1, source_target_pairs={{0,2},{1,3},{2,0},{3,1},{4,6},{5,7},{6,4},{7,5},{8,10},{9,11},{10,... | collective-permute-start | bytes 786440 | tf_op jit(solution)/shard_map/ppermute | solution.py:214
  64.4 27.9 %collective-permute-start.15 = (bf16[256,512]{1,0:T(8,128)(2,1)S(1)}, bf16[256,512]{1,0:T(8,128)(2,1)S(1)}, u32[]{:S(2)}, u32[]{:S(2)}) collective-permute-start(bf16[256,512]{1,0:T(8,128)(2,1)S(1)} %slice.40), channel_id=1, source_target_pairs={{0,1},{1,0},{2,3},{3,2},{4,5},{5,4},{6,7},{7,6},{8,9},{9,8},{10,11... | collective-permute-start | bytes 786440 | tf_op jit(solution)/shard_map/ppermute | solution.py:213
  79.4 30.2 %collective-permute-start.4 = (bf16[256,1024]{1,0:T(8,128)(2,1)S(1)}, bf16[256,1024]{1,0:T(8,128)(2,1)S(1)}, u32[]{:S(2)}, u32[]{:S(2)}) collective-permute-start(bf16[256,1024]{1,0:T(8,128)(2,1)S(1)} %get-tuple-element.26), channel_id=1, source_target_pairs={{0,1},{1,0},{2,3},{3,2},{4,5},{5,4},{6,7},{7,6},{8,9},{9,8},{10,11... | collective-permute-start | bytes 1572872 | tf_op jit(solution)/shard_map/ppermute | solution.py:213
  90.8 48.0 %copy-start = (bf16[1,2048,256]{2,1,0:T(8,128)(2,1)S(1)}, bf16[1,2048,256]{2,1,0:T(8,128)(2,1)}, u32[]{:S(2)}) copy-start(bf16[1,2048,256]{2,1,0:T(8,128)(2,1)} %param.13) | copy-start | bytes 3145732
  90.8 20.4 %collective-permute-start.5 = (bf16[256,1024]{1,0:T(8,128)(2,1)S(1)}, bf16[256,1024]{1,0:T(8,128)(2,1)S(1)}, u32[]{:S(2)}, u32[]{:S(2)}) collective-permute-start(bf16[256,1024]{1,0:T(8,128)(2,1)S(1)} %get-tuple-element.28), channel_id=1, source_target_pairs={{0,2},{1,3},{2,0},{3,1},{4,6},{5,7},{6,4},{7,5},{8,10},{9,11},{10,... | collective-permute-start | bytes 1572872 | tf_op jit(solution)/shard_map/ppermute | solution.py:214
  106.8 14.9 %collective-permute-start.16 = (bf16[256,1024]{1,0:T(8,128)(2,1)S(1)}, bf16[256,1024]{1,0:T(8,128)(2,1)S(1)}, u32[]{:S(2)}, u32[]{:S(2)}) collective-permute-start(bf16[256,1024]{1,0:T(8,128)(2,1)S(1)} %get-tuple-element.36), channel_id=1, source_target_pairs={{0,1},{1,0},{2,3},{3,2},{4,5},{5,4},{6,7},{7,6},{8,9},{9,8},{10,11... | collective-permute-start | bytes 1572872 | tf_op jit(solution)/shard_map/ppermute | solution.py:213
  107.5 31.4 %copy-start.5 = (bf16[2048,256]{1,0:T(8,128)(2,1)}, bf16[2048,256]{1,0:T(8,128)(2,1)S(1)}, u32[]{:S(2)}) copy-start(bf16[2048,256]{1,0:T(8,128)(2,1)S(1)} %collective-permute-done.8.h1) | copy-start | bytes 3145732
  107.5 14.9 %collective-permute-start.17 = (bf16[256,1024]{1,0:T(8,128)(2,1)S(1)}, bf16[256,1024]{1,0:T(8,128)(2,1)S(1)}, u32[]{:S(2)}, u32[]{:S(2)}) collective-permute-start(bf16[256,1024]{1,0:T(8,128)(2,1)S(1)} %get-tuple-element.38), channel_id=1, source_target_pairs={{0,2},{1,3},{2,0},{3,1},{4,6},{5,7},{6,4},{7,5},{8,10},{9,11},{10,... | collective-permute-start | bytes 1572872 | tf_op jit(solution)/shard_map/ppermute | solution.py:214
  108.6 30.2 %copy-start.6 = (bf16[2048,256]{1,0:T(8,128)(2,1)}, bf16[2048,256]{1,0:T(8,128)(2,1)S(1)}, u32[]{:S(2)}) copy-start(bf16[2048,256]{1,0:T(8,128)(2,1)S(1)} %collective-permute-done.9.h2) | copy-start | bytes 3145732
  108.6 24.9 %collective-permute-start.10 = (bf16[1024,256]{1,0:T(8,128)(2,1)S(1)}, bf16[1024,256]{1,0:T(8,128)(2,1)S(1)}, u32[]{:S(2)}, u32[]{:S(2)}) collective-permute-start(bf16[1024,256]{1,0:T(8,128)(2,1)S(1)} %slice.37), channel_id=1, source_target_pairs={{0,2},{1,3},{2,0},{3,1},{4,6},{5,7},{6,4},{7,5},{8,10},{9,11},{10,... | collective-permute-start | bytes 1572872 | tf_op jit(solution)/shard_map/ppermute | solution.py:214
  109.7 25.4 %collective-permute-start.11 = (bf16[1024,256]{1,0:T(8,128)(2,1)S(1)}, bf16[1024,256]{1,0:T(8,128)(2,1)S(1)}, u32[]{:S(2)}, u32[]{:S(2)}) collective-permute-start(bf16[1024,256]{1,0:T(8,128)(2,1)S(1)} %slice.38), channel_id=1, source_target_pairs={{0,1},{1,0},{2,3},{3,2},{4,5},{5,4},{6,7},{7,6},{8,9},{9,8},{10,11... | collective-permute-start | bytes 1572872 | tf_op jit(solution)/shard_map/ppermute | solution.py:213
  111.3 27.5 %collective-permute-start.6 = (bf16[128,1024]{1,0:T(8,128)(2,1)S(1)}, bf16[128,1024]{1,0:T(8,128)(2,1)S(1)}, u32[]{:S(2)}, u32[]{:S(2)}) collective-permute-start(bf16[128,1024]{1,0:T(8,128)(2,1)S(1)} %get-tuple-element.29), channel_id=1, source_target_pairs={{0,2},{1,3},{2,0},{3,1},{4,6},{5,7},{6,4},{7,5},{8,10},{9,11},{10,... | collective-permute-start | bytes 786440 | tf_op jit(solution)/shard_map/ppermute | solution.py:214
  121.8 17.1 %collective-permute-start.7 = (bf16[128,1024]{1,0:T(8,128)(2,1)S(1)}, bf16[128,1024]{1,0:T(8,128)(2,1)S(1)}, u32[]{:S(2)}, u32[]{:S(2)}) collective-permute-start(bf16[128,1024]{1,0:T(8,128)(2,1)S(1)} %get-tuple-element.30), channel_id=1, source_target_pairs={{0,1},{1,0},{2,3},{3,2},{4,5},{5,4},{6,7},{7,6},{8,9},{9,8},{10,11... | collective-permute-start | bytes 786440 | tf_op jit(solution)/shard_map/ppermute | solution.py:213
  122.3 34.3 %copy-start.4 = (s32[128,2]{0,1:T(2,128)S(1)}, s32[128,2]{0,1:T(2,128)}, u32[]{:S(2)}) copy-start(s32[128,2]{0,1:T(2,128)} %param.7) | copy-start | bytes 3076
  122.4 19.3 %collective-permute-start.18 = (bf16[128,1024]{1,0:T(8,128)(2,1)S(1)}, bf16[128,1024]{1,0:T(8,128)(2,1)S(1)}, u32[]{:S(2)}, u32[]{:S(2)}) collective-permute-start(bf16[128,1024]{1,0:T(8,128)(2,1)S(1)} %get-tuple-element.39), channel_id=1, source_target_pairs={{0,2},{1,3},{2,0},{3,1},{4,6},{5,7},{6,4},{7,5},{8,10},{9,11},{10,... | collective-permute-start | bytes 786440 | tf_op jit(solution)/shard_map/ppermute | solution.py:214
  133.6 8.2 %collective-permute-start.19 = (bf16[128,1024]{1,0:T(8,128)(2,1)S(1)}, bf16[128,1024]{1,0:T(8,128)(2,1)S(1)}, u32[]{:S(2)}, u32[]{:S(2)}) collective-permute-start(bf16[128,1024]{1,0:T(8,128)(2,1)S(1)} %get-tuple-element.40), channel_id=1, source_target_pairs={{0,1},{1,0},{2,3},{3,2},{4,5},{5,4},{6,7},{7,6},{8,9},{9,8},{10,11... | collective-permute-start | bytes 786440 | tf_op jit(solution)/shard_map/ppermute | solution.py:213
